TPU v7x, 512 devices: a whole 4x4x16 slice. The times are simulated.
512 devices in a mesh: row: 8 (over x_hi, y), col: 32 (over x_lo, z), head: 2 (over core).
Axes of the slice: x: 4 (x_hi: 2, x_lo: 2; x = x_hi * 2 + x_lo), y: 4, z: 16, core: 2. Of those that a mesh axis runs over, the one named last changes fastest.
Arguments:
- pair: bfloat16 [32, 4096, 128], P('row', 'col'), may hold values from -6 to 6
- layer_norm_gain: float32 [128], replicated, may hold values from 0.1 to 1.9
- w_proj: bfloat16 [128, 512], P(None, 'head'), may hold values from -0.5 to 0.5
- w_out: bfloat16 [128, 128], P('head'), may hold values from -0.5 to 0.5
- tri_bias: bfloat16 [4, 4096, 4096], P('head', 'col', 'row'), may hold values from -6 to 300
- active: int32 [16, 16], replicated, may hold values from 0 to 1, as said below
- d_out: bfloat16 [32, 4096, 128], P('row', 'col'), may hold values from -6 to 6
Outputs:
- out: bfloat16 [32, 4096, 128], P('row', 'col', 'head')
- pair_gradient: bfloat16 [32, 4096, 128], P('row', 'col')
Inputs may be any that keep to these rules, and one draw needn't show every extreme that they name: Entry [a, b] is 1 where key tile b is computed for query tile a; the table is symmetric and every tile is active with itself.
All inputs are finite; a program needn't handle non-finite values.
Results may differ from a plain program's by a relative error of at most 0.02.
Values may be sent and summed in bfloat16 or wider, within the bound.
No kernel may reach another device: no remote copies, remote signals or barrier semaphores. Data moves between devices by JAX's collectives and lax.ppermute only.
A program may use at most 64 MiB of HBM per device.

v0:
```python
import math
import jax
import jax.numpy as jnp
from jax import lax
from jax.sharding import PartitionSpec as P

DH = 32
TILE = 256
EPS = 1e-05
NEG = -1e30


def tile_onehot(first, count, tiles_total):
    index = (first + jnp.arange(count, dtype=jnp.int32)) // TILE
    return (index[:, None] == jnp.arange(tiles_total, dtype=jnp.int32)[None, :]).astype(jnp.float32)


def per_device(pair, layer_norm_gain, w_proj, w_out, tri_bias, active, d_out):
    rows, cols, width = pair.shape
    heads = w_out.shape[0] // DH
    scale = DH ** (-0.5)
    tiles_total = active.shape[0]
    x = pair.astype(jnp.float32)
    channel_average = jnp.mean(x, axis=-1, keepdims=True)
    centered_input = x - channel_average
    inverse_deviation = lax.rsqrt(
        jnp.mean(centered_input * centered_input, axis=-1, keepdims=True) + EPS
    )
    standardized_input = centered_input * inverse_deviation
    normalized_pair = (standardized_input * layer_norm_gain).astype(jnp.bfloat16)
    proj = jnp.einsum("rjc,cf->rjf", normalized_pair, w_proj, preferred_element_type=jnp.float32)
    proj = proj.reshape(rows, cols, heads, 4, DH)
    query = (proj[:, :, :, 0] * scale).astype(jnp.bfloat16)
    kv_local = proj[:, :, :, 1:3].astype(jnp.bfloat16).reshape(rows, cols, heads * 2 * DH)
    gate = jax.nn.sigmoid(proj[:, :, :, 3])
    col_start = lax.axis_index("col") * cols
    row_active = jnp.dot(tile_onehot(col_start, cols, tiles_total), active.astype(jnp.float32))
    gathered = lax.all_gather(kv_local, "col", axis=1, tiled=True)

    def block_parts(keys_values, piece, offset, first, step):
        bias_blk = lax.dynamic_slice_in_dim(piece, offset, step, 2)
        kv_blk = lax.dynamic_slice_in_dim(keys_values, first, step, 1).reshape(
            rows, step, heads, 2, DH
        )
        mask = jnp.dot(row_active, tile_onehot(first, step, tiles_total).T) > 0.5
        return (bias_blk, kv_blk[:, :, :, 0], kv_blk[:, :, :, 1], mask)

    def scores(key_blk, bias_blk, mask):
        score = jnp.einsum("rjhd,rkhd->rhjk", query, key_blk, preferred_element_type=jnp.float32)
        score = score + bias_blk[None].astype(jnp.float32)
        return jnp.where(mask[None, None], score, NEG)

    start_state = (
        jnp.full((rows, heads, cols), NEG, jnp.float32),
        jnp.zeros((rows, heads, cols), jnp.float32),
        jnp.zeros((rows, heads, cols, DH), jnp.float32),
    )
    piece = lax.all_gather(tri_bias, "row", axis=2, tiled=True)
    length = piece.shape[2]
    step = math.gcd(length, 2 * TILE)

    def forward_one_block(number, inner):
        offset = number * step
        bias_blk, key_blk, value_blk, mask = block_parts(gathered, piece, offset, offset, step)

        def forward_update(carry):
            run_max, run_sum, acc = carry
            score = scores(key_blk, bias_blk, mask)
            new_max = jnp.maximum(run_max, jnp.max(score, axis=-1))
            weights = jnp.where(mask[None, None], jnp.exp(score - new_max[..., None]), 0.0)
            factor = jnp.exp(run_max - new_max)
            run_sum = run_sum * factor + jnp.sum(weights, axis=-1)
            acc = acc * factor[..., None] + jnp.einsum(
                "rhjk,rkhd->rhjd",
                weights.astype(jnp.bfloat16),
                value_blk,
                preferred_element_type=jnp.float32,
            )
            return (new_max, run_sum, acc)

        return lax.cond(jnp.any(mask), forward_update, lambda carry: carry, inner)

    run_max, run_sum, acc = lax.fori_loop(0, length // step, forward_one_block, start_state)
    lse = run_max + jnp.log(run_sum)
    attended = jnp.transpose(acc / run_sum[..., None], (0, 2, 1, 3))
    gated = (gate * attended).astype(jnp.bfloat16).reshape(rows, cols, heads * DH)
    partial_out = jnp.einsum("rjf,fc->rjc", gated, w_out, preferred_element_type=jnp.float32)
    out = lax.psum_scatter(
        partial_out.astype(jnp.bfloat16), "head", scatter_dimension=2, tiled=True
    )
    d_go = jnp.einsum("rjc,fc->rjf", d_out, w_out, preferred_element_type=jnp.float32).reshape(
        rows, cols, heads, DH
    )
    d_o = d_go * gate
    delta = jnp.transpose(jnp.sum(d_o * attended, axis=-1), (0, 2, 1))
    grad_out = d_o.astype(jnp.bfloat16)
    d_gate = d_go * attended * gate * (1.0 - gate)
    gathered_back = lax.all_gather(kv_local, "col", axis=1, tiled=True)

    def backward_piece(state, piece):
        length = piece.shape[2]
        step = math.gcd(length, 2 * TILE)

        def backward_one_block(number, inner):
            offset = number * step
            first = offset
            bias_blk, key_blk, value_blk, mask = block_parts(
                gathered_back, piece, offset, first, step
            )

            def backward_update(carry):
                dq_acc, dkv_acc = carry
                score = scores(key_blk, bias_blk, mask)
                prob = jnp.where(mask[None, None], jnp.exp(score - lse[..., None]), 0.0)
                d_value = jnp.einsum(
                    "rhjk,rjhd->rkhd",
                    prob.astype(jnp.bfloat16),
                    grad_out,
                    preferred_element_type=jnp.float32,
                )
                d_prob = jnp.einsum(
                    "rjhd,rkhd->rhjk", grad_out, value_blk, preferred_element_type=jnp.float32
                )
                d_score = (prob * (d_prob - delta[..., None])).astype(jnp.bfloat16)
                dq_acc = dq_acc + jnp.einsum(
                    "rhjk,rkhd->rhjd", d_score, key_blk, preferred_element_type=jnp.float32
                )
                d_key = jnp.einsum(
                    "rhjk,rjhd->rkhd", d_score, query, preferred_element_type=jnp.float32
                )
                both = jnp.stack([d_key, d_value], axis=3).reshape(rows, step, heads * 2 * DH)
                current = lax.dynamic_slice_in_dim(dkv_acc, first, step, 1)
                dkv_acc = lax.dynamic_update_slice_in_dim(dkv_acc, current + both, first, 1)
                return (dq_acc, dkv_acc)

            return lax.cond(jnp.any(mask), backward_update, lambda carry: carry, inner)

        return lax.fori_loop(0, length // step, backward_one_block, state)

    back_state = (
        jnp.zeros((rows, heads, cols, DH), jnp.float32),
        jnp.zeros(gathered_back.shape, jnp.float32),
    )
    dq_acc, dkv_acc = backward_piece(
        back_state, lax.all_gather(tri_bias, "row", axis=2, tiled=True)
    )
    dkv_own = lax.psum_scatter(
        dkv_acc.astype(jnp.bfloat16), "col", scatter_dimension=1, tiled=True
    ).astype(jnp.float32)
    dkv_own = dkv_own.reshape(rows, cols, heads, 2, DH)
    d_query = jnp.transpose(dq_acc, (0, 2, 1, 3)) * scale
    d_proj = jnp.stack([d_query, dkv_own[:, :, :, 0], dkv_own[:, :, :, 1], d_gate], axis=3)
    d_proj = d_proj.astype(jnp.bfloat16).reshape(rows, cols, heads * 4 * DH)
    d_norm = jnp.einsum("rjf,cf->rjc", d_proj, w_proj, preferred_element_type=jnp.float32)
    d_norm = lax.psum(d_norm.astype(jnp.bfloat16), "head").astype(jnp.float32)
    input_gradient = d_norm * layer_norm_gain
    pair_gradient = inverse_deviation * (
        input_gradient
        - jnp.mean(input_gradient, axis=-1, keepdims=True)
        - standardized_input * jnp.mean(input_gradient * standardized_input, axis=-1, keepdims=True)
    )
    pair_gradient = pair_gradient.astype(jnp.bfloat16)
    return (out, pair_gradient)


def solution(mesh):
    in_specs = (
        P("row", "col", None),
        P(),
        P(None, "head"),
        P("head", None),
        P("head", "col", "row"),
        P(),
        P("row", "col", None),
    )
    out_specs = (P("row", "col", "head"), P("row", "col", None))
    return jax.shard_map(
        per_device, mesh=mesh, in_specs=in_specs, out_specs=out_specs, check_vma=False
    )
```

profile of v0, /device:TPU:1, one launch (start us, length us, event | category | flops | bytes accessed | tf_op | source)
XLA Modules:
  0.0 569.7 jit_solution(15667866155526611855)
XLA Ops:
  7.2 1.8 copy.41
  9.1 1.0 convert_reduce_fusion
  10.2 1.1 fusion.36
  11.3 1.3 fusion.38
  13.9 71.6 %all-gather.5.cloned.1.call-done = bf16[2,128,4096]{1,2,0:T(8,128)(2,1)} async-done(((bf16[2,128,512]{1,2,0:T(8,128)(2,1)}), bf16[2,128,4096]{1,2,0:T(8,128)(2,1)}) %all-gather.5.cloned.1.call-update) | async-done | bytes 2097168 | tf_op jit(solution)/shard_map/all_gather | solution.py:58
  85.5 123.1 %all-gather.3.cloned.1.call-done = bf16[4,4096,128]{1,2,0:T(8,128)(2,1)} async-done(((bf16[4,128,128]{1,2,0:T(8,128)(2,1)}), bf16[4,4096,128]{1,2,0:T(8,128)(2,1)}) %all-gather.3.cloned.1.call-update) | async-done | bytes 4194320 | tf_op jit(solution)/shard_map/all_gather | solution.py:38
  208.6 28.2 %while.36 = (s32[]{:T(128)}, f32[4,2,128]{2,1,0:T(2,128)S(1)}, f32[4,2,128]{2,1,0:T(2,128)S(1)}, f32[4,2,128,32]{2,3,1,0:T(8,128)S(1)}, bf16[128,16]{0,1:T(8,128...) while((s32[]{:T(128)}, f32[4,2,128]{2,1,0:T(2,128)S(1)}, ...), condition=%wide.region_8.9_spmd, body=%wide.region_2.8_spmd.sunk | while | flops 76367872 | bytes 10887453 | solution.py:83
  208.6 0.9 fusion.83
  210.1 4.1 conditional.4
  210.1 1.1 constant_dynamic-slice_fusion
  211.2 1.0 dynamic-slice_convert_fusion
  214.2 0.9 fusion.83
  215.7 0.9 fusion.83
  217.2 0.9 fusion.83
  218.6 4.1 conditional.4
  218.6 1.1 constant_dynamic-slice_fusion
  219.7 1.0 dynamic-slice_convert_fusion
  222.7 0.9 fusion.83
  224.2 4.1 conditional.4
  224.2 1.1 constant_dynamic-slice_fusion
  225.3 1.0 dynamic-slice_convert_fusion
  228.3 0.9 fusion.83
  229.8 0.9 fusion.83
  231.2 4.1 conditional.4
  231.2 1.1 constant_dynamic-slice_fusion
  232.3 1.0 dynamic-slice_convert_fusion
  235.3 0.9 fusion.83
  236.9 4.2 broadcast_in_dim.98
  241.2 41.5 %while.37 = (s32[]{:T(128)}, f32[4,2,128,32]{2,3,1,0:T(8,128)S(1)}, f32[4,4096,128]{1,2,0:T(8,128)}, bf16[128,16]{0,1:T(8,128)(2,1)S(1)}, bf16[4,4096,128]{1,2,0...) while((s32[]{:T(128)}, f32[4,2,128,32]{2,3,1,0:T(8,128)S(1)}, ...), condition=%wide.region_15.16_spmd, body=%wide.region_11.15_spmd.sunk | while | flops 174899200 | bytes 21643568 | solution.py:138
  241.2 0.9 fusion.85
  242.7 7.3 %conditional.5 = ((f32[4,2,128,32]{2,3,1,0:T(8,128)S(1)}, f32[4,4096,128]{1,2,0:T(8,128)})) conditional(s32[]{:T(128)} %convert_element_type.174, (f32[4,2,128,32]{2,3,1,0:T(8,128)S(1)}, f32[4,4096,128]{1,2,0:T(8,128)}) %tuple.125, (pred[128,512]{0,1:T(8,128)(4,1)S(1)}, s32[]{:T(128)}, bf16[4,4096,128]{1,2,0:T(8,128)(2,1)}, ...), branch_computations={%region_13.13_spmd, %region_14.14_spmd} | conditional | flops 172654592 | bytes 21569606 | solution.py:136
  242.7 1.1 constant_dynamic-slice_fusion.1
  243.8 1.0 dynamic-slice_convert_fusion.1
  247.6 2.4 constant_dynamic-update-slice_fusion
  250.0 0.9 fusion.85
  251.6 0.9 fusion.85
  253.2 0.9 fusion.85
  254.7 7.3 %conditional.5 = ((f32[4,2,128,32]{2,3,1,0:T(8,128)S(1)}, f32[4,4096,128]{1,2,0:T(8,128)})) conditional(s32[]{:T(128)} %convert_element_type.174, (f32[4,2,128,32]{2,3,1,0:T(8,128)S(1)}, f32[4,4096,128]{1,2,0:T(8,128)}) %tuple.125, (pred[128,512]{0,1:T(8,128)(4,1)S(1)}, s32[]{:T(128)}, bf16[4,4096,128]{1,2,0:T(8,128)(2,1)}, ...), branch_computations={%region_13.13_spmd, %region_14.14_spmd} | conditional | flops 172654592 | bytes 21569606 | solution.py:136
  254.8 1.1 constant_dynamic-slice_fusion.1
  255.8 1.0 dynamic-slice_convert_fusion.1
  259.6 2.4 constant_dynamic-update-slice_fusion
  262.0 0.9 fusion.85
  263.5 7.2 %conditional.5 = ((f32[4,2,128,32]{2,3,1,0:T(8,128)S(1)}, f32[4,4096,128]{1,2,0:T(8,128)})) conditional(s32[]{:T(128)} %convert_element_type.174, (f32[4,2,128,32]{2,3,1,0:T(8,128)S(1)}, f32[4,4096,128]{1,2,0:T(8,128)}) %tuple.125, (pred[128,512]{0,1:T(8,128)(4,1)S(1)}, s32[]{:T(128)}, bf16[4,4096,128]{1,2,0:T(8,128)(2,1)}, ...), branch_computations={%region_13.13_spmd, %region_14.14_spmd} | conditional | flops 172654592 | bytes 21569606 | solution.py:136
  263.6 1.1 constant_dynamic-slice_fusion.1
  264.6 1.0 dynamic-slice_convert_fusion.1
  268.4 2.4 constant_dynamic-update-slice_fusion
  270.8 0.9 fusion.85
  272.4 0.9 fusion.85
  273.9 7.2 %conditional.5 = ((f32[4,2,128,32]{2,3,1,0:T(8,128)S(1)}, f32[4,4096,128]{1,2,0:T(8,128)})) conditional(s32[]{:T(128)} %convert_element_type.174, (f32[4,2,128,32]{2,3,1,0:T(8,128)S(1)}, f32[4,4096,128]{1,2,0:T(8,128)}) %tuple.125, (pred[128,512]{0,1:T(8,128)(4,1)S(1)}, s32[]{:T(128)}, bf16[4,4096,128]{1,2,0:T(8,128)(2,1)}, ...), branch_computations={%region_13.13_spmd, %region_14.14_spmd} | conditional | flops 172654592 | bytes 21569606 | solution.py:136
  273.9 1.1 constant_dynamic-slice_fusion.1
  275.0 1.0 dynamic-slice_convert_fusion.1
  278.8 2.4 constant_dynamic-update-slice_fusion
  281.2 0.9 fusion.85
  282.7 6.0 %convert_element_type.115 = bf16[4,4096,128]{1,2,0:T(8,128)(2,1)} convert(f32[4,4096,128]{1,2,0:T(8,128)} %get-tuple-element.755) | non-fusion elementwise | flops 2097152 | bytes 12582912 | tf_op jit(solution)/shard_map/convert_element_type | solution.py:148
  288.7 7.5 %copy.50 = bf16[4,4096,128]{2,0,1:T(4,128)(2,1)} copy(bf16[4,4096,128]{1,2,0:T(8,128)(2,1)} %convert_element_type.115) | data formatting | bytes 8388608
  296.2 4.9 copy.58
  301.2 183.6 %reduce-scatter.7.cloned.1.call-done = bf16[128,512]{1,0:T(8,128)(2,1)} async-done(((bf16[4096,512]{1,0:T(8,128)(2,1)}), bf16[128,512]{1,0:T(8,128)(2,1)}) %reduce-scatter.7.cloned.1.call-update) | async-done | bytes 131088
  484.8 0.9 reshape.164
  485.9 0.9 convolution_convert_fusion
  486.9 0.9 convolution_convert_fusion.1
  487.8 52.9 %all-reduce.2.cloned.1.call-done = bf16[4,128,128]{2,1,0:T(8,128)(2,1)} async-done(((bf16[4,128,128]{2,1,0:T(8,128)(2,1)}), bf16[4,128,128]{2,1,0:T(8,128)(2,1)}) %all-reduce.2.cloned.1.call-update) | async-done | bytes 131088 | tf_op jit(solution)/shard_map/psum | solution.py:155
  540.7 1.3 fusion.37
  542.0 1.9 fusion.35
  543.9 19.3 %reduce-scatter.5.cloned.1.call-done = bf16[4,128,64]{1,2,0:T(8,128)(2,1)} async-done(((bf16[4,128,128]{1,2,0:T(8,128)(2,1)}), bf16[4,128,64]{1,2,0:T(8,128)(2,1)}) %reduce-scatter.5.cloned.1.call-update) | async-done | bytes 65552 | tf_op jit(solution)/shard_map/reduce_scatter | solution.py:88
  (115 shorter events, 20.6 us)
Async XLA Ops:
  7.2 6.5 %copy-start = (bf16[4,128,128]{2,1,0:T(8,128)(2,1)S(1)}, bf16[4,128,128]{2,1,0:T(8,128)(2,1)}, u32[]{:S(2)}) copy-start(bf16[4,128,128]{2,1,0:T(8,128)(2,1)} %param.21) | copy-start | bytes 393220
  7.2 6.3 %copy-start.5 = (s32[16,16]{1,0:T(8,128)S(1)}, s32[16,16]{1,0:T(8,128)}, u32[]{:S(2)}) copy-start(s32[16,16]{1,0:T(8,128)} %param.20) | copy-start | bytes 3076
  7.2 6.5 %copy-start.3 = (bf16[64,128]{1,0:T(8,128)(2,1)S(1)}, bf16[64,128]{1,0:T(8,128)(2,1)}, u32[]{:S(2)}) copy-start(bf16[64,128]{1,0:T(8,128)(2,1)} %param.18) | copy-start | bytes 49156
  7.2 78.3 %all-gather.5.cloned.1.call-start = ((), (), s32[]{:S(2)}) async-start(), calls=%async_computation.3 | async-start | bytes 2359296 | tf_op jit(solution)/shard_map/all_gather | solution.py:58
  9.1 199.5 %all-gather.3.cloned.1.call-start = ((), (), s32[]{:S(2)}) async-start(), calls=%async_computation.2 | async-start | bytes 4325376 | tf_op jit(solution)/shard_map/all_gather | solution.py:38
  13.4 471.4 %reduce-scatter.7.cloned.1.call-start = ((), (), s32[]{:S(2)}) async-start(), calls=%async_computation.6 | async-start | bytes 4325376
  301.0 184.9 %copy-start.2 = (bf16[128,256]{1,0:T(8,128)(2,1)S(1)}, bf16[128,256]{1,0:T(8,128)(2,1)}, u32[]{:S(2)}) copy-start(bf16[128,256]{1,0:T(8,128)(2,1)} %param.17) | copy-start | bytes 196612
  301.1 239.6 %copy-start.1 = (bf16[4,128,128]{2,1,0:T(8,128)(2,1)S(1)}, bf16[4,128,128]{2,1,0:T(8,128)(2,1)}, u32[]{:S(2)}) copy-start(bf16[4,128,128]{2,1,0:T(8,128)(2,1)} %param.15) | copy-start | bytes 393220
  301.1 239.6 %copy-start.4 = (f32[128]{0:T(128)S(1)}, f32[128]{0:T(128)}, u32[]{:S(2)}) copy-start(f32[128]{0:T(128)} %param.16) | copy-start | bytes 1540
  301.1 239.6 %all-reduce.2.cloned.1.call-start = ((), (), s32[]{:S(2)}) async-start(), calls=%async_computation.5 | async-start | bytes 262144 | tf_op jit(solution)/shard_map/psum | solution.py:155
  486.9 76.3 %reduce-scatter.5.cloned.1.call-start = ((), (), s32[]{:S(2)}) async-start(), calls=%async_computation.4 | async-start | bytes 196608 | tf_op jit(solution)/shard_map/reduce_scatter | solution.py:88
Sparse Core Ops, SparseCore 0:
  11.2 74.2 all-gather.4
  88.0 120.4 all-gather.2
  301.2 183.5 reduce-scatter.6
  488.1 52.5 all-reduce.1
  543.9 19.2 reduce-scatter.4
where the time goes:
time: 572 us; the launch traced here: 570 us
  waiting for transfers between devices  451 us (79%)
  matrix products  33.4 us (6%)
  other arithmetic  31.8 us (6%)
  local copies, waits for them, and re-layouts  29.2 us (5%)
  between operations  14 us (2%)
  loops' own time  10.5 us (2%)
    unnamed x6, waiting for transfers between devices  184 us
    all_gather x1, waiting for transfers between devices, per_device(): gathered = lax.all_gather(kv_local, 'col', axis=1, tiled=True)  123 us
    all_gather x1, waiting for transfers between devices, per_device(): piece = lax.all_gather(tri_bias, 'row', axis=2, tiled=True)  71.6 us
    psum x1, waiting for transfers between devices, per_device(): d_norm = lax.psum(d_norm.astype(jnp.bfloat16), 'head').astype(jnp.float32)  52.9 us
    reduce_scatter x1, waiting for transfers between devices, per_device(): lax.psum_scatter(partial_out.astype(jnp.bfloat16), 'head', scatter_dimens...  19.3 us
    unnamed x17, local copies, waits for them, and re-layouts  15.3 us
    dot_general x16, matrix products, block_parts(): mask = jnp.dot(row_active, tile_onehot(first, step, tiles_total).T) > 0.5  14.3 us
  transfers between devices with their start and end apart: 5, of which 5 were waited for; matrix products, arithmetic and copies ran while one was open for 2% of the time, Pallas kernels for 0%

commit v1 on v0

--- a/solution.py
+++ b/solution.py
@@ -8,6 +8,10 @@
 TILE = 256
 EPS = 1e-05
 NEG = -1e30
+
+
+def rest_the_area(obj, ax_name="head"):
+    return lax.all_gather(obj, ax_name).sum(axis=0)
 
 
 def tile_onehot(first, count, tiles_total):
@@ -152,7 +156,7 @@
     d_proj = jnp.stack([d_query, dkv_own[:, :, :, 0], dkv_own[:, :, :, 1], d_gate], axis=3)
     d_proj = d_proj.astype(jnp.bfloat16).reshape(rows, cols, heads * 4 * DH)
     d_norm = jnp.einsum("rjf,cf->rjc", d_proj, w_proj, preferred_element_type=jnp.float32)
-    d_norm = lax.psum(d_norm.astype(jnp.bfloat16), "head").astype(jnp.float32)
+    d_norm = rest_the_area(d_norm.astype(jnp.bfloat16)).astype(jnp.float32)
     input_gradient = d_norm * layer_norm_gain
     pair_gradient = inverse_deviation * (
         input_gradient

time: 572 us -> 531 us (0.928)
  waiting for transfers between devices: 451 us -> 386 us
  blocking collectives: 0 us -> 23.2 us
    psum x1 -> x0, waiting for transfers between devices: 52.9 us -> none  [per_device(): d_norm = lax.psum(d_norm.astype(jnp.bfloat16), 'head').astype(jnp.float32)]
    all_gather x0 -> x1, blocking collectives: none -> 23.2 us  [rest_the_area(): return lax.all_gather(obj, ax_name).sum(axis=0)]
    reduce_scatter x1, waiting for transfers between devices: 19.3 us -> 8.6 us  [per_device(): lax.psum_scatter(partial_out.astype(jnp.bfloat16), 'head', scatter_dimens...]
    unnamed x6 -> x5, waiting for transfers between devices: 184 us -> 183 us
  transfers between devices with their start and end apart: 5 -> 4, of which waited for: 5 -> 4; matrix products, arithmetic and copies ran while one was open for 2% -> 2% of each run, Pallas kernels for 0% -> 0%
where the time goes in v1:
time: 531 us; the launch traced here: 529 us
  waiting for transfers between devices  386 us (73%)
  matrix products  34 us (6%)
  other arithmetic  30 us (6%)
  local copies, waits for them, and re-layouts  29.2 us (5%)
  blocking collectives  23.2 us (4%)
  between operations  14 us (3%)
  loops' own time  12.2 us (2%)
    unnamed x5, waiting for transfers between devices  183 us
    all_gather x1, waiting for transfers between devices, per_device(): gathered = lax.all_gather(kv_local, 'col', axis=1, tiled=True)  123 us
    all_gather x1, waiting for transfers between devices, per_device(): piece = lax.all_gather(tri_bias, 'row', axis=2, tiled=True)  71.6 us
    all_gather x1, blocking collectives, rest_the_area(): return lax.all_gather(obj, ax_name).sum(axis=0)  23.2 us
    dot_general x16, matrix products, block_parts(): mask = jnp.dot(row_active, tile_onehot(first, step, tiles_total).T) > 0.5  15.5 us
    unnamed x17, local copies, waits for them, and re-layouts  15.2 us
  transfers between devices with their start and end apart: 4, of which 4 were waited for; matrix products, arithmetic and copies ran while one was open for 2% of the time, Pallas kernels for 0%

profile of v1, /device:TPU:1, one launch (start us, length us, event | category | flops | bytes accessed | tf_op | source)
XLA Modules:
  0.0 528.9 jit_solution(17225977970667857129)
XLA Ops:
  7.2 1.8 copy.41
  9.1 1.0 convert_reduce_fusion
  10.2 1.1 fusion.36
  11.3 1.3 fusion.38
  13.9 71.6 %all-gather.6.cloned.1.call-done = bf16[2,128,4096]{1,2,0:T(8,128)(2,1)} async-done(((bf16[2,128,512]{1,2,0:T(8,128)(2,1)}), bf16[2,128,4096]{1,2,0:T(8,128)(2,1)}) %all-gather.6.cloned.1.call-update) | async-done | bytes 2097168 | tf_op jit(solution)/shard_map/all_gather | solution.py:62
  85.5 123.1 %all-gather.4.cloned.1.call-done = bf16[4,4096,128]{1,2,0:T(8,128)(2,1)} async-done(((bf16[4,128,128]{1,2,0:T(8,128)(2,1)}), bf16[4,4096,128]{1,2,0:T(8,128)(2,1)}) %all-gather.4.cloned.1.call-update) | async-done | bytes 4194320 | tf_op jit(solution)/shard_map/all_gather | solution.py:42
  208.6 29.9 %while.36 = (s32[]{:T(128)}, f32[4,2,128]{2,1,0:T(2,128)S(1)}, f32[4,2,128]{2,1,0:T(2,128)S(1)}, f32[4,2,128,32]{2,3,1,0:T(8,128)S(1)}, bf16[128,16]{0,1:T(8,128...) while((s32[]{:T(128)}, f32[4,2,128]{2,1,0:T(2,128)S(1)}, ...), condition=%wide.region_8.9_spmd, body=%wide.region_2.8_spmd.sunk | while | flops 76367872 | bytes 10887453 | solution.py:87
  208.6 1.0 fusion.83
  210.3 4.1 conditional.4
  210.3 1.1 constant_dynamic-slice_fusion
  211.4 1.0 dynamic-slice_convert_fusion
  214.4 1.0 fusion.83
  216.1 1.0 fusion.83
  217.8 1.0 fusion.83
  219.5 4.1 conditional.4
  219.5 1.1 constant_dynamic-slice_fusion
  220.6 1.0 dynamic-slice_convert_fusion
  223.6 1.0 fusion.83
  225.3 4.1 conditional.4
  225.3 1.1 constant_dynamic-slice_fusion
  226.4 1.0 dynamic-slice_convert_fusion
  229.3 1.0 fusion.83
  231.1 1.0 fusion.83
  232.7 4.1 conditional.4
  232.8 1.1 constant_dynamic-slice_fusion
  233.8 1.0 dynamic-slice_convert_fusion
  236.8 1.0 fusion.83
  238.7 4.3 broadcast_in_dim.98
  242.9 42.6 %while.37 = (s32[]{:T(128)}, f32[4,2,128,32]{2,3,1,0:T(8,128)S(1)}, f32[4,4096,128]{1,2,0:T(8,128)}, bf16[128,16]{0,1:T(8,128)(2,1)S(1)}, bf16[4,4096,128]{1,2,0...) while((s32[]{:T(128)}, f32[4,2,128,32]{2,3,1,0:T(8,128)S(1)}, ...), condition=%wide.region_15.16_spmd, body=%wide.region_11.15_spmd.sunk | while | flops 174899200 | bytes 21643568 | solution.py:142
  242.9 1.0 fusion.85
  244.6 7.3 %conditional.5 = ((f32[4,2,128,32]{2,3,1,0:T(8,128)S(1)}, f32[4,4096,128]{1,2,0:T(8,128)})) conditional(s32[]{:T(128)} %convert_element_type.176, (f32[4,2,128,32]{2,3,1,0:T(8,128)S(1)}, f32[4,4096,128]{1,2,0:T(8,128)}) %tuple.125, (pred[128,512]{0,1:T(8,128)(4,1)S(1)}, s32[]{:T(128)}, bf16[4,4096,128]{1,2,0:T(8,128)(2,1)}, ...), branch_computations={%region_13.13_spmd, %region_14.14_spmd} | conditional | flops 172654592 | bytes 21569606 | solution.py:140
  244.6 1.1 constant_dynamic-slice_fusion.1
  245.7 1.0 dynamic-slice_convert_fusion.1
  246.7 0.8 fusion.20
  249.5 2.4 constant_dynamic-update-slice_fusion
  251.9 1.0 fusion.85
  253.6 1.0 fusion.85
  255.4 1.0 fusion.85
  257.0 7.2 %conditional.5 = ((f32[4,2,128,32]{2,3,1,0:T(8,128)S(1)}, f32[4,4096,128]{1,2,0:T(8,128)})) conditional(s32[]{:T(128)} %convert_element_type.176, (f32[4,2,128,32]{2,3,1,0:T(8,128)S(1)}, f32[4,4096,128]{1,2,0:T(8,128)}) %tuple.125, (pred[128,512]{0,1:T(8,128)(4,1)S(1)}, s32[]{:T(128)}, bf16[4,4096,128]{1,2,0:T(8,128)(2,1)}, ...), branch_computations={%region_13.13_spmd, %region_14.14_spmd} | conditional | flops 172654592 | bytes 21569606 | solution.py:140
  257.1 1.1 constant_dynamic-slice_fusion.1
  258.1 1.0 dynamic-slice_convert_fusion.1
  261.9 2.4 constant_dynamic-update-slice_fusion
  264.3 1.0 fusion.85
  265.9 7.3 %conditional.5 = ((f32[4,2,128,32]{2,3,1,0:T(8,128)S(1)}, f32[4,4096,128]{1,2,0:T(8,128)})) conditional(s32[]{:T(128)} %convert_element_type.176, (f32[4,2,128,32]{2,3,1,0:T(8,128)S(1)}, f32[4,4096,128]{1,2,0:T(8,128)}) %tuple.125, (pred[128,512]{0,1:T(8,128)(4,1)S(1)}, s32[]{:T(128)}, bf16[4,4096,128]{1,2,0:T(8,128)(2,1)}, ...), branch_computations={%region_13.13_spmd, %region_14.14_spmd} | conditional | flops 172654592 | bytes 21569606 | solution.py:140
  266.0 1.1 constant_dynamic-slice_fusion.1
  267.0 1.0 dynamic-slice_convert_fusion.1
  268.0 0.8 fusion.20
  270.8 2.4 constant_dynamic-update-slice_fusion
  273.2 1.0 fusion.85
  274.9 1.0 fusion.85
  276.6 7.2 %conditional.5 = ((f32[4,2,128,32]{2,3,1,0:T(8,128)S(1)}, f32[4,4096,128]{1,2,0:T(8,128)})) conditional(s32[]{:T(128)} %convert_element_type.176, (f32[4,2,128,32]{2,3,1,0:T(8,128)S(1)}, f32[4,4096,128]{1,2,0:T(8,128)}) %tuple.125, (pred[128,512]{0,1:T(8,128)(4,1)S(1)}, s32[]{:T(128)}, bf16[4,4096,128]{1,2,0:T(8,128)(2,1)}, ...), branch_computations={%region_13.13_spmd, %region_14.14_spmd} | conditional | flops 172654592 | bytes 21569606 | solution.py:140
  276.6 1.1 constant_dynamic-slice_fusion.1
  277.7 1.0 dynamic-slice_convert_fusion.1
  281.5 2.4 constant_dynamic-update-slice_fusion
  283.9 1.0 fusion.85
  285.6 6.0 %convert_element_type.117 = bf16[4,4096,128]{1,2,0:T(8,128)(2,1)} convert(f32[4,4096,128]{1,2,0:T(8,128)} %get-tuple-element.755) | non-fusion elementwise | flops 2097152 | bytes 12582912 | tf_op jit(solution)/shard_map/convert_element_type | solution.py:152
  291.6 7.5 %copy.50 = bf16[4,4096,128]{2,0,1:T(4,128)(2,1)} copy(bf16[4,4096,128]{1,2,0:T(8,128)(2,1)} %convert_element_type.117) | data formatting | bytes 8388608
  299.0 4.8 copy.58
  304.0 0.9 convolution_convert_fusion.1
  304.9 182.8 %reduce-scatter.7.cloned.1.call-done = bf16[128,512]{1,0:T(8,128)(2,1)} async-done(((bf16[4096,512]{1,0:T(8,128)(2,1)}), bf16[128,512]{1,0:T(8,128)(2,1)}) %reduce-scatter.7.cloned.1.call-update) | async-done | bytes 131088
  487.7 0.9 reshape.165
  489.1 23.2 %all-gather = bf16[8,128,128]{2,1,0:T(8,128)(2,1)S(1)} all-gather(bf16[4,128,128]{2,1,0:T(8,128)(2,1)S(1)} %convolution_convert_fusion), channel_id=2, replica_groups=mesh['row'=8,'col'=32,'head'=2] {'head'}, dimensions={0}, use_global_device_ids=true | all-gather | bytes 393216 | tf_op jit(solution)/shard_map/all_gather | solution.py:14
  512.7 1.0 fusion.35
  513.7 8.6 %reduce-scatter.5.cloned.1.call-done = bf16[4,128,64]{1,2,0:T(8,128)(2,1)} async-done(((bf16[4,128,128]{1,2,0:T(8,128)(2,1)}), bf16[4,128,64]{1,2,0:T(8,128)(2,1)}) %reduce-scatter.5.cloned.1.call-update) | async-done | bytes 65552 | tf_op jit(solution)/shard_map/reduce_scatter | solution.py:92
  (114 shorter events, 19.6 us)
Async XLA Ops:
  7.2 6.5 %copy-start = (bf16[4,128,128]{2,1,0:T(8,128)(2,1)S(1)}, bf16[4,128,128]{2,1,0:T(8,128)(2,1)}, u32[]{:S(2)}) copy-start(bf16[4,128,128]{2,1,0:T(8,128)(2,1)} %param.21) | copy-start | bytes 393220
  7.2 6.3 %copy-start.5 = (s32[16,16]{1,0:T(8,128)S(1)}, s32[16,16]{1,0:T(8,128)}, u32[]{:S(2)}) copy-start(s32[16,16]{1,0:T(8,128)} %param.20) | copy-start | bytes 3076
  7.2 6.5 %copy-start.3 = (bf16[64,128]{1,0:T(8,128)(2,1)S(1)}, bf16[64,128]{1,0:T(8,128)(2,1)}, u32[]{:S(2)}) copy-start(bf16[64,128]{1,0:T(8,128)(2,1)} %param.18) | copy-start | bytes 49156
  7.2 78.3 %all-gather.6.cloned.1.call-start = ((), (), s32[]{:S(2)}) async-start(), calls=%async_computation.3 | async-start | bytes 2359296 | tf_op jit(solution)/shard_map/all_gather | solution.py:62
  9.1 199.5 %all-gather.4.cloned.1.call-start = ((), (), s32[]{:S(2)}) async-start(), calls=%async_computation.2 | async-start | bytes 4325376 | tf_op jit(solution)/shard_map/all_gather | solution.py:42
  13.4 474.3 %reduce-scatter.7.cloned.1.call-start = ((), (), s32[]{:S(2)}) async-start(), calls=%async_computation.5 | async-start | bytes 4325376
  303.9 185.0 %copy-start.2 = (bf16[128,256]{1,0:T(8,128)(2,1)S(1)}, bf16[128,256]{1,0:T(8,128)(2,1)}, u32[]{:S(2)}) copy-start(bf16[128,256]{1,0:T(8,128)(2,1)} %param.17) | copy-start | bytes 196612
  303.9 208.5 %copy-start.1 = (bf16[4,128,128]{2,1,0:T(8,128)(2,1)S(1)}, bf16[4,128,128]{2,1,0:T(8,128)(2,1)}, u32[]{:S(2)}) copy-start(bf16[4,128,128]{2,1,0:T(8,128)(2,1)} %param.15) | copy-start | bytes 393220
  303.9 208.5 %copy-start.4 = (f32[128]{0:T(128)S(1)}, f32[128]{0:T(128)}, u32[]{:S(2)}) copy-start(f32[128]{0:T(128)} %param.16) | copy-start | bytes 1540
  303.9 218.4 %reduce-scatter.5.cloned.1.call-start = ((), (), s32[]{:S(2)}) async-start(), calls=%async_computation.4 | async-start | bytes 196608 | tf_op jit(solution)/shard_map/reduce_scatter | solution.py:92
Sparse Core Ops, SparseCore 0:
  11.2 74.2 all-gather.5
  88.0 120.4 all-gather.3
  304.0 183.6 reduce-scatter.6
  490.9 31.4 reduce-scatter.4
